TPU v7x, 32 devices: a whole 2x2x4 slice. The times are simulated.
32 devices in a mesh: fsdp: 16 (over z, y, x), seq: 2 (over core).
Axes of the slice: x: 2, y: 2, z: 4, core: 2. Of those that a mesh axis runs over, the one named last changes fastest.
Arguments:
- latents: bfloat16 [16, 1024, 1152], P('fsdp', 'seq'), may hold values from -3 to 3
- captions: bfloat16 [16, 120, 1152], P('fsdp'), may hold values from -3 to 3
- conditions: float32 [16, 6912], P('fsdp'), may hold values from -0.75 to 0.75
- table: bfloat16 [6, 1152], P(None, 'fsdp'), may hold values from -0.75 to 0.75
- w_qkv: bfloat16 [1152, 3456], P('fsdp'), may hold values from -0.1875 to 0.1875
- w_out: bfloat16 [1152, 1152], P('fsdp'), may hold values from -1.5 to 1.5
- w_cross_q: bfloat16 [1152, 1152], P('fsdp'), may hold values from -0.1875 to 0.1875
- w_cross_kv: bfloat16 [1152, 2304], P('fsdp'), may hold values from -0.1875 to 0.1875
- w_cross_out: bfloat16 [1152, 1152], P('fsdp'), may hold values from -0.5 to 0.5
- w_fc_in: bfloat16 [1152, 4608], P('fsdp'), may hold values from -0.1875 to 0.1875
- w_fc_out: bfloat16 [4608, 1152], P('fsdp'), may hold values from -0.09375 to 0.09375
- cotangent: bfloat16 [16, 1024, 1152], P('fsdp', 'seq'), may hold values from -3 to 3
Outputs:
- output: bfloat16 [16, 1024, 1152], P('fsdp', 'seq')
- grad_latents: float32 [16, 1024, 1152], P('fsdp', 'seq')
- grad_captions: float32 [16, 120, 1152], P('fsdp')
- grad_conditions: float32 [16, 6912], P('fsdp')
- grad_mlp_shift: float32 [16, 1152], P('fsdp')
- grad_table: float32 [6, 1152], P(None, 'fsdp')
- grad_w_qkv: float32 [1152, 3456], P('fsdp')
- grad_w_out: float32 [1152, 1152], P('fsdp')
- grad_w_cross_q: float32 [1152, 1152], P('fsdp')
- grad_w_cross_kv: float32 [1152, 2304], P('fsdp')
- grad_w_cross_out: float32 [1152, 1152], P('fsdp')
- grad_w_fc_in: float32 [1152, 4608], P('fsdp')
- grad_w_fc_out: float32 [4608, 1152], P('fsdp')
All inputs are finite; a program needn't handle non-finite values.
Results may differ from a plain program's by a relative error of at most 0.03.
Values may be sent and summed in bfloat16 or wider, within the bound.
A program may use at most 224 MiB of HBM per device.

v0:
```python
import math

import jax
import jax.numpy as jnp
from jax import lax
from jax.sharding import PartitionSpec as P

H = 16
HD = 72


eps_norm = 1e-06


def layer_norm(values):
    average = jnp.mean(values, axis=-1, keepdims=True)
    centred = values - average
    variance = jnp.mean(centred * centred, axis=-1, keepdims=True)
    return centred * lax.rsqrt(variance + eps_norm)


def modulate(values, shift_rows, scale_rows):
    return layer_norm(values) * (1.0 + scale_rows[:, None, :]) + shift_rows[:, None, :]


def gelu_tanh(values):
    return jax.nn.gelu(values, approximate=True)


def product(left_side, right_side):
    return jnp.dot(left_side, right_side, preferred_element_type=jnp.float32)


def outer_sum(left_side, right_side):
    return lax.dot_general(
        left_side, right_side, (((0,), (0,)), ((), ())), preferred_element_type=jnp.float32
    )


def back_product(left_side, right_side):
    return lax.dot_general(
        left_side, right_side, (((1,), (1,)), ((), ())), preferred_element_type=jnp.float32
    )


def split_heads(values):
    return values.reshape(values.shape[0], values.shape[1], H, HD)


def attention_scores(queries, key_rows):
    return jnp.einsum(
        "sqhd,skhd->shqk",
        split_heads(queries),
        split_heads(key_rows),
        preferred_element_type=jnp.float32,
    ) * (1.0 / math.sqrt(HD))


def attention_forward(queries, key_rows, value_rows):
    scores = attention_scores(queries, key_rows)
    row_max = jnp.max(scores, axis=-1, keepdims=True)
    exponent = jnp.exp(scores - row_max)
    denominator = jnp.sum(exponent, axis=-1, keepdims=True)
    probability = (exponent / denominator).astype(jnp.bfloat16)
    log_total = row_max + jnp.log(denominator)
    mixed_rows = jnp.einsum(
        "shqk,skhd->sqhd", probability, split_heads(value_rows), preferred_element_type=jnp.float32
    )
    return (mixed_rows.reshape(queries.shape).astype(jnp.bfloat16), log_total)


def score_grads(queries, key_rows, value_rows, log_total, grad_mixed, row_sums):
    probability = jnp.exp(attention_scores(queries, key_rows) - log_total)
    grad_prob = jnp.einsum(
        "sqhd,skhd->shqk",
        split_heads(grad_mixed),
        split_heads(value_rows),
        preferred_element_type=jnp.float32,
    )
    row_sums = jnp.sum(probability * grad_prob, axis=-1, keepdims=True)
    grad_scores = (probability * (grad_prob - row_sums)).astype(jnp.bfloat16)
    return (probability, grad_scores, row_sums)


def key_side(queries, key_rows, grad_mixed, probability, grad_scores):
    factor = 1.0 / math.sqrt(HD)
    grad_values = jnp.einsum(
        "shqk,sqhd->skhd",
        probability.astype(jnp.bfloat16),
        split_heads(grad_mixed),
        preferred_element_type=jnp.float32,
    )
    grad_keys = (
        jnp.einsum(
            "shqk,sqhd->skhd", grad_scores, split_heads(queries), preferred_element_type=jnp.float32
        )
        * factor
    )
    return (grad_keys.reshape(key_rows.shape), grad_values.reshape(key_rows.shape))


def query_side(key_rows, grad_scores, query_shape):
    factor = 1.0 / math.sqrt(HD)
    grad_queries = (
        jnp.einsum(
            "shqk,skhd->sqhd",
            grad_scores,
            split_heads(key_rows),
            preferred_element_type=jnp.float32,
        )
        * factor
    )
    return grad_queries.reshape(query_shape)


def attention_backward(queries, key_rows, value_rows, log_total, grad_mixed):
    probability, grad_scores, row_sums = score_grads(
        queries, key_rows, value_rows, log_total, grad_mixed, None
    )
    grad_queries = query_side(key_rows, grad_scores, queries.shape)
    grad_keys, grad_values = key_side(queries, key_rows, grad_mixed, probability, grad_scores)
    return (grad_queries, grad_keys, grad_values)


def body(
    latents,
    captions,
    conditions,
    table,
    w_qkv,
    w_out,
    w_cross_q,
    w_cross_kv,
    w_cross_out,
    w_fc_in,
    w_fc_out,
    cotangent,
):
    gathered = (
        lax.all_gather(table, "fsdp", axis=1, tiled=True),
        lax.all_gather(w_qkv, "fsdp", axis=0, tiled=True),
        lax.all_gather(w_out, "fsdp", axis=0, tiled=True),
        lax.all_gather(w_cross_q, "fsdp", axis=0, tiled=True),
        lax.all_gather(w_cross_kv, "fsdp", axis=0, tiled=True),
        lax.all_gather(w_cross_out, "fsdp", axis=0, tiled=True),
        lax.all_gather(w_fc_in, "fsdp", axis=0, tiled=True),
        lax.all_gather(w_fc_out, "fsdp", axis=0, tiled=True),
    )
    full_table, full_qkv, full_out, full_cq, full_ckv, full_co, full_fc_in, full_fc_out = gathered
    seq_count, row_count, model_width = latents.shape
    flat_rows = seq_count * row_count
    text_rows = captions.shape[1]
    modulation = full_table.astype(jnp.float32)[None] + conditions.reshape(
        seq_count, 6, model_width
    )
    shift_one, scale_one, gate_one, shift_two, scale_two, gate_two = jnp.moveaxis(modulation, 1, 0)
    residual_in = latents.astype(jnp.float32)
    normed_one, pull_one = jax.vjp(modulate, residual_in, shift_one, scale_one)
    normed_low = normed_one.astype(jnp.bfloat16).reshape(flat_rows, model_width)
    joined = (
        product(normed_low, full_qkv)
        .astype(jnp.bfloat16)
        .reshape(seq_count, row_count, 3 * model_width)
    )
    queries = joined[..., :model_width]
    all_kv = lax.all_gather(joined[..., model_width:], "seq", axis=1, tiled=True)
    all_keys = all_kv[..., :model_width]
    all_values = all_kv[..., model_width:]
    mixed_self, log_self = attention_forward(queries, all_keys, all_values)
    branch = product(mixed_self.reshape(flat_rows, model_width), full_out).reshape(
        seq_count, row_count, model_width
    )
    after_self = residual_in + gate_one[:, None] * branch
    cross_in = after_self.astype(jnp.bfloat16).reshape(flat_rows, model_width)
    cross_query = (
        product(cross_in, full_cq).astype(jnp.bfloat16).reshape(seq_count, row_count, model_width)
    )
    caption_rows = captions.reshape(seq_count * text_rows, model_width)
    cross_kv = (
        product(caption_rows, full_ckv)
        .astype(jnp.bfloat16)
        .reshape(seq_count, text_rows, 2 * model_width)
    )
    cross_keys = cross_kv[..., :model_width]
    cross_values = cross_kv[..., model_width:]
    cross_mixed, log_cross = attention_forward(cross_query, cross_keys, cross_values)
    cross_flat = cross_mixed.reshape(flat_rows, model_width)
    after_cross = after_self + product(cross_flat, full_co).reshape(
        seq_count, row_count, model_width
    )
    normed_two, pull_two = jax.vjp(modulate, after_cross, shift_two, scale_two)
    normed_two_low = normed_two.astype(jnp.bfloat16).reshape(flat_rows, model_width)
    hidden_pre = product(normed_two_low, full_fc_in)
    hidden, pull_gelu = jax.vjp(gelu_tanh, hidden_pre)
    hidden_low = hidden.astype(jnp.bfloat16)
    expanded = product(hidden_low, full_fc_out).reshape(seq_count, row_count, model_width)
    output = (after_cross + gate_two[:, None] * expanded).astype(jnp.bfloat16)
    again_full = (
        lax.all_gather(w_qkv, "fsdp", axis=0, tiled=True),
        lax.all_gather(w_out, "fsdp", axis=0, tiled=True),
        lax.all_gather(w_cross_q, "fsdp", axis=0, tiled=True),
        lax.all_gather(w_cross_kv, "fsdp", axis=0, tiled=True),
        lax.all_gather(w_cross_out, "fsdp", axis=0, tiled=True),
        lax.all_gather(w_fc_in, "fsdp", axis=0, tiled=True),
        lax.all_gather(w_fc_out, "fsdp", axis=0, tiled=True),
    )
    back_qkv, back_out, back_cq, back_ckv, back_co, back_fc_in, back_fc_out = again_full
    grad_out = cotangent.astype(jnp.float32)
    grad_gate_two = jnp.sum(grad_out * expanded, axis=1)
    grad_expanded = (
        (grad_out * gate_two[:, None]).astype(jnp.bfloat16).reshape(flat_rows, model_width)
    )
    grad_fc_out = outer_sum(hidden_low, grad_expanded)
    grad_hidden = back_product(grad_expanded, back_fc_out)
    grad_pre = pull_gelu(grad_hidden)[0].astype(jnp.bfloat16)
    grad_fc_in = outer_sum(normed_two_low, grad_pre)
    grad_normed_two = back_product(grad_pre, back_fc_in).reshape(seq_count, row_count, model_width)
    grad_cross_side, grad_shift_two, grad_scale_two = pull_two(grad_normed_two)
    grad_after_cross = grad_out + grad_cross_side
    grad_cross_branch = grad_after_cross.astype(jnp.bfloat16).reshape(flat_rows, model_width)
    grad_cross_out = outer_sum(cross_flat, grad_cross_branch)
    grad_cross_mixed = (
        back_product(grad_cross_branch, back_co)
        .astype(jnp.bfloat16)
        .reshape(seq_count, row_count, model_width)
    )
    grad_cq_rows, grad_cross_keys, grad_cross_values = attention_backward(
        cross_query, cross_keys, cross_values, log_cross, grad_cross_mixed
    )
    grad_cross_query = grad_cq_rows.astype(jnp.bfloat16).reshape(flat_rows, model_width)
    grad_cross_q = outer_sum(cross_in, grad_cross_query)
    grad_after_self = grad_after_cross + back_product(grad_cross_query, back_cq).reshape(
        seq_count, row_count, model_width
    )
    grad_cross_part = jnp.concatenate([grad_cross_keys, grad_cross_values], axis=-1)
    grad_gate_one = jnp.sum(grad_after_self * branch, axis=1)
    grad_branch = (
        (grad_after_self * gate_one[:, None]).astype(jnp.bfloat16).reshape(flat_rows, model_width)
    )
    grad_w_out = outer_sum(mixed_self.reshape(flat_rows, model_width), grad_branch)
    grad_mixed = (
        back_product(grad_branch, back_out)
        .astype(jnp.bfloat16)
        .reshape(seq_count, row_count, model_width)
    )
    grad_queries, grad_keys, grad_values = attention_backward(
        queries, all_keys, all_values, log_self, grad_mixed
    )
    grad_kv_own = lax.psum_scatter(
        jnp.concatenate([grad_keys, grad_values], axis=-1), "seq", scatter_dimension=1, tiled=True
    )
    grad_joined = (
        jnp.concatenate([grad_queries, grad_kv_own], axis=-1)
        .astype(jnp.bfloat16)
        .reshape(flat_rows, 3 * model_width)
    )
    grad_w_qkv = outer_sum(normed_low, grad_joined)
    grad_normed_one = back_product(grad_joined, back_qkv).reshape(seq_count, row_count, model_width)
    grad_in_side, grad_shift_one, grad_scale_one = pull_one(grad_normed_one)
    grad_latents = grad_after_self + grad_in_side
    grad_modulation = jnp.stack(
        [
            grad_shift_one,
            grad_scale_one,
            grad_gate_one,
            grad_shift_two,
            grad_scale_two,
            grad_gate_two,
        ],
        axis=1,
    )
    summed_cross, summed_mod = lax.psum((grad_cross_part, grad_modulation), "seq")
    grad_cross_low = summed_cross.astype(jnp.bfloat16).reshape(
        seq_count * text_rows, 2 * model_width
    )
    grad_cross_kv = outer_sum(caption_rows, grad_cross_low)
    grad_captions = back_product(grad_cross_low, back_ckv).reshape(
        seq_count, text_rows, model_width
    )
    grad_conditions = summed_mod.reshape(seq_count, 6 * model_width)
    grad_mlp_shift = summed_mod[:, 3]
    grad_table_full = jnp.sum(summed_mod, axis=0)
    column_parts = (
        lax.psum_scatter(grad_w_qkv, "seq", scatter_dimension=1, tiled=True),
        lax.psum_scatter(grad_w_out, "seq", scatter_dimension=1, tiled=True),
        lax.psum_scatter(grad_cross_q, "seq", scatter_dimension=1, tiled=True),
        lax.psum_scatter(grad_cross_out, "seq", scatter_dimension=1, tiled=True),
        lax.psum_scatter(grad_fc_in, "seq", scatter_dimension=1, tiled=True),
        lax.psum_scatter(grad_fc_out, "seq", scatter_dimension=1, tiled=True),
    )
    owned_parts = (
        lax.psum_scatter(grad_table_full, "fsdp", scatter_dimension=1, tiled=True),
        lax.psum_scatter(grad_cross_kv, "fsdp", scatter_dimension=0, tiled=True),
        lax.psum_scatter(column_parts[0], "fsdp", scatter_dimension=0, tiled=True),
        lax.psum_scatter(column_parts[1], "fsdp", scatter_dimension=0, tiled=True),
        lax.psum_scatter(column_parts[2], "fsdp", scatter_dimension=0, tiled=True),
        lax.psum_scatter(column_parts[3], "fsdp", scatter_dimension=0, tiled=True),
        lax.psum_scatter(column_parts[4], "fsdp", scatter_dimension=0, tiled=True),
        lax.psum_scatter(column_parts[5], "fsdp", scatter_dimension=0, tiled=True),
    )
    owned_table, owned_kv_cross = (owned_parts[0], owned_parts[1])
    owned_qkv, owned_out, owned_cq, owned_co, owned_fc_in, owned_fc_out = (
        lax.all_gather(owned_parts[2], "seq", axis=1, tiled=True),
        lax.all_gather(owned_parts[3], "seq", axis=1, tiled=True),
        lax.all_gather(owned_parts[4], "seq", axis=1, tiled=True),
        lax.all_gather(owned_parts[5], "seq", axis=1, tiled=True),
        lax.all_gather(owned_parts[6], "seq", axis=1, tiled=True),
        lax.all_gather(owned_parts[7], "seq", axis=1, tiled=True),
    )
    return (
        output,
        grad_latents,
        grad_captions,
        grad_conditions,
        grad_mlp_shift,
        owned_table,
        owned_qkv,
        owned_out,
        owned_cq,
        owned_kv_cross,
        owned_co,
        owned_fc_in,
        owned_fc_out,
    )


def solution(mesh):
    in_specs = (
        P("fsdp", "seq", None),
        P("fsdp", None, None),
        P("fsdp", None),
        P(None, "fsdp"),
        P("fsdp", None),
        P("fsdp", None),
        P("fsdp", None),
        P("fsdp", None),
        P("fsdp", None),
        P("fsdp", None),
        P("fsdp", None),
        P("fsdp", "seq", None),
    )
    out_specs = (
        P("fsdp", "seq", None),
        P("fsdp", "seq", None),
        P("fsdp", None, None),
        P("fsdp", None),
        P("fsdp", None),
        P(None, "fsdp"),
        P("fsdp", None),
        P("fsdp", None),
        P("fsdp", None),
        P("fsdp", None),
        P("fsdp", None),
        P("fsdp", None),
        P("fsdp", None),
    )
    return jax.shard_map(body, mesh=mesh, in_specs=in_specs, out_specs=out_specs, check_vma=False)
```

profile of v0, /device:TPU:0, one launch (start us, length us, event | category | flops | bytes accessed | tf_op | source)
XLA Modules:
  0.0 1993.7 jit_solution(4036822462009302347)
XLA Ops:
  9.6 43.3 %all-gather = bf16[16,72,6]{1,2,0:T(8,128)(2,1)S(1)} all-gather(bf16[1,72,6]{1,2,0:T(8,128)(2,1)} %bitcast.282), channel_id=1, replica_groups=mesh['fsdp'=16,'seq'=2] {'fsdp'}, dimensions={0}, use_global_device_ids=true | all-gather | bytes 14688 | tf_op jit(solution)/shard_map/all_gather | solution.py:140
  55.1 67.4 %all-gather.17.cloned.1.call-done = bf16[1152,3456]{1,0:T(8,128)(2,1)} async-done(((bf16[72,3456]{1,0:T(8,128)(2,1)}), bf16[1152,3456]{1,0:T(8,128)(2,1)}) %all-gather.17.cloned.1.call-update) | async-done | bytes 7962640 | tf_op jit(solution)/shard_map/all_gather | solution.py:141
  138.2 71.1 %all-gather.23.cloned.1.call-done = bf16[1152,2304]{1,0:T(8,128)(2,1)} async-done(((bf16[72,2304]{1,0:T(8,128)(2,1)}), bf16[1152,2304]{1,0:T(8,128)(2,1)}) %all-gather.23.cloned.1.call-update) | async-done | bytes 5308432 | tf_op jit(solution)/shard_map/all_gather | solution.py:144
  237.8 15.0 multiply_reduce_fusion.1
  252.9 14.5 fusion
  267.4 13.7 fusion.45
  297.7 60.4 %all-gather.25.cloned.1.call-done = bf16[1152,1152]{1,0:T(8,128)(2,1)} async-done(((bf16[72,1152]{1,0:T(8,128)(2,1)}), bf16[1152,1152]{1,0:T(8,128)(2,1)}) %all-gather.25.cloned.1.call-update) | async-done | bytes 2654224 | tf_op jit(solution)/shard_map/all_gather | solution.py:143
  368.6 55.2 %all-gather.27.cloned.1.call-done = bf16[1152,1152]{1,0:T(8,128)(2,1)} async-done(((bf16[72,1152]{1,0:T(8,128)(2,1)}), bf16[1152,1152]{1,0:T(8,128)(2,1)}) %all-gather.27.cloned.1.call-update) | async-done | bytes 2654224 | tf_op jit(solution)/shard_map/all_gather | solution.py:145
  430.3 128.8 %all-gather.29.cloned.1.call-done = bf16[1152,4608]{1,0:T(8,128)(2,1)} async-done(((bf16[72,4608]{1,0:T(8,128)(2,1)}), bf16[1152,4608]{1,0:T(8,128)(2,1)}) %all-gather.29.cloned.1.call-update) | async-done | bytes 10616848 | tf_op jit(solution)/shard_map/all_gather | solution.py:146
  583.4 110.2 %all-gather.31.cloned.1.call-done = bf16[4608,1152]{1,0:T(8,128)(2,1)} async-done(((bf16[288,1152]{1,0:T(8,128)(2,1)}), bf16[4608,1152]{1,0:T(8,128)(2,1)}) %all-gather.31.cloned.1.call-update) | async-done | bytes 10616848 | tf_op jit(solution)/shard_map/all_gather | solution.py:147
  693.6 15.3 fusion.13
  711.8 13.6 fusion.83
  737.9 18.7 fusion.32
  779.7 24.2 %multiply_reduce_fusion = (f32[16,512]{1,0:T(8,128)S(1)}, f32[16,512,1024]{2,1,0:T(8,128)}) fusion(f32[16,512,1024]{2,1,0:T(8,128)} %get-tuple-element.106, f32[16,512]{1,0:T(8,128)S(1)} %log_add_fusion, bf16[512,16,72]{0,2,1:T(8,128)(2,1)} %bitcast.252, bf16[1024,16,72]{0,2,1:T(8,128)(2,1)S(1)} %bitcast.251), kind=kOutput, calls=%fused_computation.1 | convolution fusion | flops 1241505792 | bytes 70713344 | tf_op jit(solution)/shard_map/sqhd,skhd->shqk/dot_general | solution.py:74
  804.0 28.3 %multiply_convert_fusion = bf16[16,512,1024]{2,1,0:T(8,128)(2,1)} fusion(f32[16,512,1024]{2,1,0:T(8,128)} %get-tuple-element.115, f32[16,512,1024]{2,1,0:T(8,128)} %get-tuple-element.106, f32[16,512]{1,0:T(8,128)S(1)} %get-tuple-element.114, f32[16,512]{1,0:T(8,128)S(1)} %log_add_fusion), kind=kLoop, calls=%fused_computation | loop fusion | flops 41943040 | bytes 83951616 | tf_op jit(solution)/shard_map/convert_element_type | solution.py:81
  841.1 16.3 fusion.2
  933.1 201.4 %reduce-scatter.42.cloned.1.call-done = f32[288,576]{1,0:T(8,128)} async-done(((f32[4608,576]{1,0:T(8,128)}), f32[288,576]{1,0:T(8,128)}) %reduce-scatter.42.cloned.1.call-update) | async-done | bytes 663568
  1137.2 184.4 %reduce-scatter.34.cloned.1.call-done = f32[72,2304]{1,0:T(8,128)} async-done(((f32[1152,2304]{1,0:T(8,128)}), f32[72,2304]{1,0:T(8,128)}) %reduce-scatter.34.cloned.1.call-update) | async-done | bytes 663568 | tf_op jit(solution)/shard_map/reduce_scatter | solution.py:298
  1321.7 27.3 %reduce-scatter.24.cloned.1.call-done = f32[1152,1728]{0,1:T(8,128)} async-done(((f32[1152,3456]{0,1:T(8,128)}), f32[1152,1728]{0,1:T(8,128)}) %reduce-scatter.24.cloned.1.call-update) | async-done | bytes 7962640 | tf_op jit(solution)/shard_map/reduce_scatter | solution.py:284
  1399.3 12.8 copy.125
  1414.0 191.2 %all-reduce.9.cloned.1.call-done = (f32[1152,576]{0,1:T(8,128)}, f32[1152,576]{0,1:T(8,128)}, f32[1152,576]{0,1:T(8,128)}) async-done(((f32[1152,576]{0,1:T(8,128)}, f32[1152,576]{0,1:T(8,128)}, f32[1152,576]{0,1:T(8,128)}), (f32[1152,576]{0,1:T(8,128)}, f32[1152,576]{0,1:T(8,128)}, f32[1152,576]{0,1:T(8,128)})) %all-reduce.9.cloned.1.call-update) | async-done | bytes 7962640
  1619.9 75.9 %all-reduce = f32[6,1152]{1,0:T(8,128)S(1)} all-reduce(f32[6,1152]{1,0:T(8,128)S(1)} %bitcast.280), channel_id=3, replica_groups=mesh['fsdp'=16,'seq'=2] {'fsdp'}, use_global_device_ids=true, to_apply=%region_23.0.clone | all-reduce | flops 6912 | bytes 55296
  1706.8 91.2 %reduce-scatter.38.cloned.1.call-done = f32[72,1728]{1,0:T(8,128)} async-done(((f32[1152,1728]{1,0:T(8,128)}), f32[72,1728]{1,0:T(8,128)}) %reduce-scatter.38.cloned.1.call-update) | async-done | bytes 497680
  1804.5 181.1 %reduce-scatter.40.cloned.1.call-done = f32[72,2304]{1,0:T(8,128)} async-done(((f32[1152,2304]{1,0:T(8,128)}), f32[72,2304]{1,0:T(8,128)}) %reduce-scatter.40.cloned.1.call-update) | async-done | bytes 663568
  (281 shorter events, 316.0 us)
Async XLA Ops:
  7.2 202.1 %copy-start = (bf16[1,120,1152]{2,1,0:T(8,128)(2,1)S(1)}, bf16[1,120,1152]{2,1,0:T(8,128)(2,1)}, u32[]{:S(2)}) copy-start(bf16[1,120,1152]{2,1,0:T(8,128)(2,1)} %param.13) | copy-start | bytes 829444
  7.2 115.4 %all-gather.17.cloned.1.call-start = ((), (), s32[]{:S(2)}) async-start(), calls=%async_computation.11 | async-start | bytes 8460288 | tf_op jit(solution)/shard_map/all_gather | solution.py:141
  7.9 201.3 %all-gather.23.cloned.1.call-start = ((), (), s32[]{:S(2)}) async-start(), calls=%async_computation.14 | async-start | bytes 5640192 | tf_op jit(solution)/shard_map/all_gather | solution.py:144
  8.7 215.7 %all-gather.19.cloned.1.call-start = ((), (), s32[]{:S(2)}) async-start(), calls=%async_computation.12 | async-start | bytes 7077888 | tf_op jit(solution)/shard_map/all_gather | solution.py:166
  134.7 157.6 %all-gather.21.cloned.1.call-start = ((), (), s32[]{:S(2)}) async-start(), calls=%async_computation.13 | async-start | bytes 2820096 | tf_op jit(solution)/shard_map/all_gather | solution.py:142
  135.3 222.8 %all-gather.25.cloned.1.call-start = ((), (), s32[]{:S(2)}) async-start(), calls=%async_computation.15 | async-start | bytes 2820096 | tf_op jit(solution)/shard_map/all_gather | solution.py:143
  135.9 288.0 %all-gather.27.cloned.1.call-start = ((), (), s32[]{:S(2)}) async-start(), calls=%async_computation.16 | async-start | bytes 2820096 | tf_op jit(solution)/shard_map/all_gather | solution.py:145
  136.5 422.7 %all-gather.29.cloned.1.call-start = ((), (), s32[]{:S(2)}) async-start(), calls=%async_computation.17 | async-start | bytes 11280384 | tf_op jit(solution)/shard_map/all_gather | solution.py:146
  137.2 556.4 %all-gather.31.cloned.1.call-start = ((), (), s32[]{:S(2)}) async-start(), calls=%async_computation.18 | async-start | bytes 11280384 | tf_op jit(solution)/shard_map/all_gather | solution.py:147
  138.0 747.5 %reduce-scatter.36.cloned.1.call-start = ((), (), s32[]{:S(2)}) async-start(), calls=%async_computation.27 | async-start | bytes 31850496 | tf_op jit(solution)/shard_map/reduce_scatter | solution.py:289
  583.3 314.8 %reduce-scatter.32.cloned.1.call-start = ((), (), s32[]{:S(2)}) async-start(), calls=%async_computation.24 | async-start | bytes 31850496 | tf_op jit(solution)/shard_map/reduce_scatter | solution.py:288
  725.4 186.6 %reduce-scatter.22.cloned.1.call-start = ((), (), s32[]{:S(2)}) async-start(), calls=%async_computation.19 | async-start | bytes 14155776 | tf_op jit(solution)/shard_map/reduce_scatter | solution.py:249
  865.0 62.4 %reduce-scatter.28.cloned.1.call-start = ((), (), s32[]{:S(2)}) async-start(), calls=%async_computation.22 | async-start | bytes 7962624 | tf_op jit(solution)/shard_map/reduce_scatter | solution.py:286
  870.6 56.8 %reduce-scatter.30.cloned.1.call-start = ((), (), s32[]{:S(2)}) async-start(), calls=%async_computation.23 | async-start | bytes 7962624 | tf_op jit(solution)/shard_map/reduce_scatter | solution.py:287
  877.5 55.6 %reduce-scatter.26.cloned.1.call-start = ((), (), s32[]{:S(2)}) async-start(), calls=%async_computation.21 | async-start | bytes 7962624 | tf_op jit(solution)/shard_map/reduce_scatter | solution.py:285
  885.4 249.1 %reduce-scatter.42.cloned.1.call-start = ((), (), s32[]{:S(2)}) async-start(), calls=%async_computation.31 | async-start | bytes 12533760
  898.0 423.6 %reduce-scatter.34.cloned.1.call-start = ((), (), s32[]{:S(2)}) async-start(), calls=%async_computation.25 | async-start | bytes 11280384 | tf_op jit(solution)/shard_map/reduce_scatter | solution.py:298
  898.6 450.4 %reduce-scatter.24.cloned.1.call-start = ((), (), s32[]{:S(2)}) async-start(), calls=%async_computation.20 | async-start | bytes 23887872 | tf_op jit(solution)/shard_map/reduce_scatter | solution.py:284
  927.4 677.8 %all-reduce.9.cloned.1.call-start = ((), (), s32[]{:S(2)}) async-start(), calls=%async_computation.32 | async-start | bytes 15925248
  933.1 769.2 %all-gather.35.cloned.1.call-start = ((), (), s32[]{:S(2)}) async-start(), calls=%async_computation.28 | async-start | bytes 2211840 | tf_op jit(solution)/shard_map/all_gather | solution.py:308
  1137.1 569.7 %all-gather.33.cloned.1.call-start = ((), (), s32[]{:S(2)}) async-start(), calls=%async_computation.26 | async-start | bytes 1990656 | tf_op jit(solution)/shard_map/all_gather | solution.py:307
  1321.6 476.3 %reduce-scatter.38.cloned.1.call-start = ((), (), s32[]{:S(2)}) async-start(), calls=%async_computation.29 | async-start | bytes 8773632
  1358.0 627.6 %reduce-scatter.40.cloned.1.call-start = ((), (), s32[]{:S(2)}) async-start(), calls=%async_computation.30 | async-start | bytes 11280384
  1802.2 183.4 %copy-start.30 = (f32[72,4608]{1,0:T(8,128)S(1)}, f32[72,4608]{1,0:T(8,128)}, u32[]{:S(2)}) copy-start(f32[72,4608]{1,0:T(8,128)} %all-gather.33.cloned.1.call-done) | copy-start | bytes 3981316
  (58 other events, 917.0 us)
Sparse Core Ops, SparseCore 0:
  10.7 111.7 all-gather.16
  125.3 83.8 all-gather.22
  211.4 12.9 all-gather.18
  226.9 65.4 all-gather.20
  294.9 63.1 all-gather.24
  360.6 63.1 all-gather.26
  426.7 132.4 all-gather.28
  561.9 131.6 all-gather.30
  695.9 29.1 reduce-scatter.35
  727.4 32.1 reduce-scatter.31
  865.1 17.5 reduce-scatter.21
  884.9 14.5 reduce-scatter.27
  901.8 14.5 reduce-scatter.29
  918.5 14.5 reduce-scatter.25
  938.8 195.6 reduce-scatter.41
  1140.2 181.3 reduce-scatter.33
  1323.9 25.0 reduce-scatter.23
  1355.3 249.8 all-reduce.8
  1607.3 8.5 all-gather.34
  1617.3 10.8 all-gather.32
  1633.9 164.0 reduce-scatter.37
  1804.4 181.1 reduce-scatter.39
where the time goes:
time: 2000 us; the launch traced here: 1990 us
  waiting for transfers between devices  1400 us (70%)
  matrix products  260 us (13%)
  blocking collectives  135 us (7%)
  local copies, waits for them, and re-layouts  111 us (6%)
  other arithmetic  71.6 us (4%)
    unnamed x26, waiting for transfers between devices  670 us
    reduce_scatter x1, waiting for transfers between devices, body(): lax.psum_scatter(column_parts[4], 'fsdp', scatter_dimension=0, tiled=True)  184 us
    all_gather x1, waiting for transfers between devices, body(): lax.all_gather(w_fc_in, 'fsdp', axis=0, tiled=True)  129 us
    all_gather x1, waiting for transfers between devices, body(): lax.all_gather(w_fc_out, 'fsdp', axis=0, tiled=True)  110 us
    unnamed x142, local copies, waits for them, and re-layouts  82.1 us
    unnamed x1, blocking collectives  75.9 us
    all_gather x1, waiting for transfers between devices, body(): lax.all_gather(w_cross_kv, 'fsdp', axis=0, tiled=True)  71.1 us
    all_gather x1, waiting for transfers between devices, body(): lax.all_gather(w_qkv, 'fsdp', axis=0, tiled=True)  67.4 us
  transfers between devices with their start and end apart: 22, of which 15 were waited for; matrix products, arithmetic and copies ran while one was open for 21% of the time, Pallas kernels for 0%

commit v1 on v0

--- a/solution.py
+++ b/solution.py
@@ -120,6 +120,107 @@
     grad_queries = query_side(key_rows, grad_scores, queries.shape)
     grad_keys, grad_values = key_side(queries, key_rows, grad_mixed, probability, grad_scores)
     return (grad_queries, grad_keys, grad_values)
+
+def bit_count(size):
+    return size.bit_length() - 1
+
+
+def swap(values, axis_name, bit):
+    size = lax.axis_size(axis_name)
+    return lax.ppermute(values, axis_name, [(i, i ^ (1 << bit)) for i in range(size)])
+
+
+def my_bit(axis_name, bit):
+    return lax.rem(lax.shift_right_logical(lax.axis_index(axis_name), jnp.int32(bit)), 2)
+
+
+def exchange_gather(values, axis_name, rotation=0):
+    bits = bit_count(lax.axis_size(axis_name))
+    held = values.reshape((1,) * bits + values.shape)
+    for step in range(bits):
+        bit = (step + rotation) % bits
+        dim = bits - 1 - bit
+        other = swap(held, axis_name, bit)
+        upper = my_bit(axis_name, bit) == 1
+        held = jnp.concatenate(
+            [jnp.where(upper, other, held), jnp.where(upper, held, other)], axis=dim
+        )
+    return held.reshape((1 << bits,) + values.shape)
+
+
+def exchange_sum_scatter(values, axis_name, rotation=0, last=jnp.float32, lead=0):
+    bits = bit_count(lax.axis_size(axis_name))
+    held = values.reshape(values.shape[:lead] + (2,) * bits + values.shape[lead + 1 :])
+    for step in range(bits):
+        bit = (bits - 1 - step + rotation) % bits
+        dim = lead + bits - 1 - bit
+        mine = my_bit(axis_name, bit)
+        kept = lax.dynamic_index_in_dim(held, mine, dim, keepdims=True)
+        other = swap(lax.dynamic_index_in_dim(held, 1 - mine, dim, keepdims=True), axis_name, bit)
+        total = kept.astype(jnp.float32) + other.astype(jnp.float32)
+        held = total.astype(last if step == bits - 1 else values.dtype)
+    return held.reshape(values.shape[:lead] + values.shape[lead + 1 :])
+
+
+def exchange_sum(values, axis_name):
+    for bit in range(bit_count(lax.axis_size(axis_name))):
+        values = values + swap(values, axis_name, bit)
+    return values
+
+
+def column_units(shard, width):
+    return [shard[:, i : i + width] for i in range(0, shard.shape[1], width)]
+
+
+def gather_units(units, rotations):
+    parts = lax.axis_size("seq")
+    share = len(units) // parts
+    stacked = jnp.stack(units).reshape((parts, share) + units[0].shape)
+    mine = lax.dynamic_index_in_dim(stacked, lax.axis_index("seq"), 0, keepdims=False)
+    gathered = jnp.stack(
+        [
+            exchange_gather(mine[i], "fsdp", rotations[i % len(rotations)])
+            for i in range(share)
+        ]
+    )
+    whole = exchange_gather(gathered, "seq")
+    return whole.reshape((len(units), whole.shape[2]) + units[0].shape)
+
+
+def scatter_units(units, rotations):
+    parts = lax.axis_size("seq")
+    share = len(units) // parts
+    stacked = jnp.stack(units).reshape((parts, share) + units[0].shape)
+    mine = exchange_sum_scatter(stacked, "seq", last=jnp.bfloat16)
+    owned = jnp.stack(
+        [
+            exchange_sum_scatter(mine[i], "fsdp", rotations[i % len(rotations)])
+            for i in range(share)
+        ]
+    )
+    whole = exchange_gather(owned, "seq")
+    return whole.reshape((len(units),) + units[0].shape[1:])
+
+
+def grad_units(grad):
+    width = grad.shape[0]
+    low = grad.astype(jnp.bfloat16)
+    devices = lax.axis_size("fsdp")
+    return [
+        piece.reshape(devices, width // devices, width) for piece in column_units(low, width)
+    ]
+
+
+ROTATIONS = ((0, 1), (2, 0), (1, 2), (0, 1))
+
+
+def in_groups(function, units):
+    size = max(4, lax.axis_size("seq"))
+    results = []
+    for number, start in enumerate(range(0, len(units), size)):
+        group = function(units[start : start + size], ROTATIONS[number % len(ROTATIONS)])
+        results.extend(group[i] for i in range(size))
+    return results
 
 
 def body(
@@ -136,17 +237,32 @@
     w_fc_out,
     cotangent,
 ):
-    gathered = (
-        lax.all_gather(table, "fsdp", axis=1, tiled=True),
-        lax.all_gather(w_qkv, "fsdp", axis=0, tiled=True),
-        lax.all_gather(w_out, "fsdp", axis=0, tiled=True),
-        lax.all_gather(w_cross_q, "fsdp", axis=0, tiled=True),
-        lax.all_gather(w_cross_kv, "fsdp", axis=0, tiled=True),
-        lax.all_gather(w_cross_out, "fsdp", axis=0, tiled=True),
-        lax.all_gather(w_fc_in, "fsdp", axis=0, tiled=True),
-        lax.all_gather(w_fc_out, "fsdp", axis=0, tiled=True),
-    )
-    full_table, full_qkv, full_out, full_cq, full_ckv, full_co, full_fc_in, full_fc_out = gathered
+    width = latents.shape[-1]
+    rows = w_out.shape[0]
+    full_table = jnp.moveaxis(exchange_gather(table, "fsdp"), 0, 1).reshape(table.shape[0], width)
+    whole_tiles = rows % 8 == 0
+    if whole_tiles:
+        pieces = in_groups(
+            gather_units,
+            column_units(w_qkv, width)
+            + [w_out, w_cross_q]
+            + column_units(w_cross_kv, width)
+            + [w_cross_out]
+            + column_units(w_fc_in, width)
+            + [w_fc_out[i : i + rows] for i in range(0, w_fc_out.shape[0], rows)],
+        )
+        square = [piece.reshape(width, width) for piece in pieces[:12]]
+        full_qkv = jnp.concatenate(square[0:3], axis=1)
+        full_out, full_cq = square[3], square[4]
+        full_ckv = jnp.concatenate(square[5:7], axis=1)
+        full_co = square[7]
+        full_fc_in = jnp.concatenate(square[8:12], axis=1)
+        full_fc_out = jnp.stack(pieces[12:], axis=1).reshape(-1, width)
+    else:
+        full_qkv, full_out, full_cq, full_ckv, full_co, full_fc_in, full_fc_out = (
+            lax.all_gather(shard, "fsdp", axis=0, tiled=True)
+            for shard in (w_qkv, w_out, w_cross_q, w_cross_kv, w_cross_out, w_fc_in, w_fc_out)
+        )
     seq_count, row_count, model_width = latents.shape
     flat_rows = seq_count * row_count
     text_rows = captions.shape[1]
@@ -163,7 +279,13 @@
         .reshape(seq_count, row_count, 3 * model_width)
     )
     queries = joined[..., :model_width]
-    all_kv = lax.all_gather(joined[..., model_width:], "seq", axis=1, tiled=True)
+    own_kv = joined[..., model_width:]
+    if whole_tiles:
+        all_kv = jnp.moveaxis(exchange_gather(own_kv, "seq"), 0, 1).reshape(
+            seq_count, -1, 2 * model_width
+        )
+    else:
+        all_kv = lax.all_gather(own_kv, "seq", axis=1, tiled=True)
     all_keys = all_kv[..., :model_width]
     all_values = all_kv[..., model_width:]
     mixed_self, log_self = attention_forward(queries, all_keys, all_values)
@@ -195,16 +317,8 @@
     hidden_low = hidden.astype(jnp.bfloat16)
     expanded = product(hidden_low, full_fc_out).reshape(seq_count, row_count, model_width)
     output = (after_cross + gate_two[:, None] * expanded).astype(jnp.bfloat16)
-    again_full = (
-        lax.all_gather(w_qkv, "fsdp", axis=0, tiled=True),
-        lax.all_gather(w_out, "fsdp", axis=0, tiled=True),
-        lax.all_gather(w_cross_q, "fsdp", axis=0, tiled=True),
-        lax.all_gather(w_cross_kv, "fsdp", axis=0, tiled=True),
-        lax.all_gather(w_cross_out, "fsdp", axis=0, tiled=True),
-        lax.all_gather(w_fc_in, "fsdp", axis=0, tiled=True),
-        lax.all_gather(w_fc_out, "fsdp", axis=0, tiled=True),
-    )
-    back_qkv, back_out, back_cq, back_ckv, back_co, back_fc_in, back_fc_out = again_full
+    back_qkv, back_out, back_cq, back_ckv = full_qkv, full_out, full_cq, full_ckv
+    back_co, back_fc_in, back_fc_out = full_co, full_fc_in, full_fc_out
     grad_out = cotangent.astype(jnp.float32)
     grad_gate_two = jnp.sum(grad_out * expanded, axis=1)
     grad_expanded = (
@@ -246,11 +360,14 @@
     grad_queries, grad_keys, grad_values = attention_backward(
         queries, all_keys, all_values, log_self, grad_mixed
     )
-    grad_kv_own = lax.psum_scatter(
-        jnp.concatenate([grad_keys, grad_values], axis=-1), "seq", scatter_dimension=1, tiled=True
+    grad_keys_own, grad_values_own = (
+        exchange_sum_scatter(
+            grad.astype(jnp.bfloat16).reshape(seq_count, -1, row_count, model_width), "seq", lead=1
+        )
+        for grad in (grad_keys, grad_values)
     )
     grad_joined = (
-        jnp.concatenate([grad_queries, grad_kv_own], axis=-1)
+        jnp.concatenate([grad_queries, grad_keys_own, grad_values_own], axis=-1)
         .astype(jnp.bfloat16)
         .reshape(flat_rows, 3 * model_width)
     )
@@ -269,7 +386,8 @@
         ],
         axis=1,
     )
-    summed_cross, summed_mod = lax.psum((grad_cross_part, grad_modulation), "seq")
+    summed_cross = exchange_sum(grad_cross_part, "seq")
+    summed_mod = exchange_sum(grad_modulation, "seq")
     grad_cross_low = summed_cross.astype(jnp.bfloat16).reshape(
         seq_count * text_rows, 2 * model_width
     )
@@ -280,33 +398,56 @@
     grad_conditions = summed_mod.reshape(seq_count, 6 * model_width)
     grad_mlp_shift = summed_mod[:, 3]
     grad_table_full = jnp.sum(summed_mod, axis=0)
-    column_parts = (
-        lax.psum_scatter(grad_w_qkv, "seq", scatter_dimension=1, tiled=True),
-        lax.psum_scatter(grad_w_out, "seq", scatter_dimension=1, tiled=True),
-        lax.psum_scatter(grad_cross_q, "seq", scatter_dimension=1, tiled=True),
-        lax.psum_scatter(grad_cross_out, "seq", scatter_dimension=1, tiled=True),
-        lax.psum_scatter(grad_fc_in, "seq", scatter_dimension=1, tiled=True),
-        lax.psum_scatter(grad_fc_out, "seq", scatter_dimension=1, tiled=True),
-    )
-    owned_parts = (
-        lax.psum_scatter(grad_table_full, "fsdp", scatter_dimension=1, tiled=True),
-        lax.psum_scatter(grad_cross_kv, "fsdp", scatter_dimension=0, tiled=True),
-        lax.psum_scatter(column_parts[0], "fsdp", scatter_dimension=0, tiled=True),
-        lax.psum_scatter(column_parts[1], "fsdp", scatter_dimension=0, tiled=True),
-        lax.psum_scatter(column_parts[2], "fsdp", scatter_dimension=0, tiled=True),
-        lax.psum_scatter(column_parts[3], "fsdp", scatter_dimension=0, tiled=True),
-        lax.psum_scatter(column_parts[4], "fsdp", scatter_dimension=0, tiled=True),
-        lax.psum_scatter(column_parts[5], "fsdp", scatter_dimension=0, tiled=True),
-    )
-    owned_table, owned_kv_cross = (owned_parts[0], owned_parts[1])
-    owned_qkv, owned_out, owned_cq, owned_co, owned_fc_in, owned_fc_out = (
-        lax.all_gather(owned_parts[2], "seq", axis=1, tiled=True),
-        lax.all_gather(owned_parts[3], "seq", axis=1, tiled=True),
-        lax.all_gather(owned_parts[4], "seq", axis=1, tiled=True),
-        lax.all_gather(owned_parts[5], "seq", axis=1, tiled=True),
-        lax.all_gather(owned_parts[6], "seq", axis=1, tiled=True),
-        lax.all_gather(owned_parts[7], "seq", axis=1, tiled=True),
-    )
+    table_rows = jnp.moveaxis(grad_table_full.reshape(6, lax.axis_size("fsdp"), -1), 1, 0)
+    owned_table = exchange_sum_scatter(table_rows, "fsdp")
+    if whole_tiles:
+        first_of_seq = (lax.axis_index("seq") == 0).astype(jnp.float32)
+        fc_out_blocks = grad_fc_out.astype(jnp.bfloat16).reshape(
+            lax.axis_size("fsdp"), -1, rows, width
+        )
+        owned = in_groups(
+            scatter_units,
+            [fc_out_blocks[:, i] for i in range(fc_out_blocks.shape[1])]
+            + grad_units(grad_fc_in)
+            + grad_units(grad_cross_out)
+            + grad_units(grad_cross_q)
+            + grad_units(grad_cross_kv * first_of_seq)
+            + grad_units(grad_w_out)
+            + grad_units(grad_w_qkv),
+        )
+        owned_fc_out = jnp.concatenate(owned[0:4], axis=0)
+        owned_fc_in = jnp.concatenate(owned[4:8], axis=1)
+        owned_co, owned_cq = owned[8], owned[9]
+        owned_kv_cross = jnp.concatenate(owned[10:12], axis=1)
+        owned_out = owned[12]
+        owned_qkv = jnp.concatenate(owned[13:16], axis=1)
+    else:
+        column_parts = (
+            lax.psum_scatter(grad_w_qkv.astype(jnp.bfloat16), "seq", scatter_dimension=1, tiled=True),
+            lax.psum_scatter(grad_w_out.astype(jnp.bfloat16), "seq", scatter_dimension=1, tiled=True),
+            lax.psum_scatter(grad_cross_q.astype(jnp.bfloat16), "seq", scatter_dimension=1, tiled=True),
+            lax.psum_scatter(grad_cross_out.astype(jnp.bfloat16), "seq", scatter_dimension=1, tiled=True),
+            lax.psum_scatter(grad_fc_in.astype(jnp.bfloat16), "seq", scatter_dimension=1, tiled=True),
+            lax.psum_scatter(grad_fc_out.astype(jnp.bfloat16), "seq", scatter_dimension=1, tiled=True),
+        )
+        owned_parts = (
+            lax.psum_scatter(grad_cross_kv.astype(jnp.bfloat16), "fsdp", scatter_dimension=0, tiled=True),
+            lax.psum_scatter(column_parts[0], "fsdp", scatter_dimension=0, tiled=True),
+            lax.psum_scatter(column_parts[1], "fsdp", scatter_dimension=0, tiled=True),
+            lax.psum_scatter(column_parts[2], "fsdp", scatter_dimension=0, tiled=True),
+            lax.psum_scatter(column_parts[3], "fsdp", scatter_dimension=0, tiled=True),
+            lax.psum_scatter(column_parts[4], "fsdp", scatter_dimension=0, tiled=True),
+            lax.psum_scatter(column_parts[5], "fsdp", scatter_dimension=0, tiled=True),
+        )
+        owned_kv_cross = owned_parts[0].astype(jnp.float32)
+        owned_qkv, owned_out, owned_cq, owned_co, owned_fc_in, owned_fc_out = (
+            lax.all_gather(owned_parts[1], "seq", axis=1, tiled=True).astype(jnp.float32),
+            lax.all_gather(owned_parts[2], "seq", axis=1, tiled=True).astype(jnp.float32),
+            lax.all_gather(owned_parts[3], "seq", axis=1, tiled=True).astype(jnp.float32),
+            lax.all_gather(owned_parts[4], "seq", axis=1, tiled=True).astype(jnp.float32),
+            lax.all_gather(owned_parts[5], "seq", axis=1, tiled=True).astype(jnp.float32),
+            lax.all_gather(owned_parts[6], "seq", axis=1, tiled=True).astype(jnp.float32),
+        )
     return (
         output,
         grad_latents,

time: 2000 us -> 1220 us (0.61)
  waiting for transfers between devices: 1400 us -> 529 us
  other arithmetic: 71.6 us -> 207 us
  blocking collectives: 135 us -> 0 us
  starting transfers between devices: 1.43 us -> 73.3 us
  local copies, waits for them, and re-layouts: 111 us -> 156 us
  matrix products: 260 us -> 238 us
    unnamed x26 -> x0, waiting for transfers between devices: 670 us -> none
    ppermute x0 -> x89, waiting for transfers between devices: none -> 529 us  [swap(): lax.ppermute(values, axis_name, [(i, i ^ 1 << bit) for i in range(size)])]
    all_gather x10 -> x0, waiting for transfers between devices: 511 us -> none  [the longest x1 129 us: body(): lax.all_gather(w_fc_in, 'fsdp', axis=0, tiled=True)]
    reduce_scatter x8 -> x0, waiting for transfers between devices: 217 us -> none  [the longest x1 184 us: body(): lax.psum_scatter(column_parts[4], 'fsdp', scatter_dimension=0, tiled=True)]
    unnamed x1 -> x0, blocking collectives: 75.9 us -> none
    ppermute x0 -> x89, starting transfers between devices: none -> 73.3 us  [swap(): lax.ppermute(values, axis_name, [(i, i ^ 1 << bit) for i in range(size)])]
    all_gather x5 -> x0, blocking collectives: 52.3 us -> none  [the longest x1 43.3 us: body(): lax.all_gather(table, 'fsdp', axis=1, tiled=True)]
    unnamed x142 -> x218, local copies, waits for them, and re-layouts: 82.1 us -> 39.5 us
  transfers between devices with their start and end apart: 22 -> 89, of which waited for: 15 -> 38; matrix products, arithmetic and copies ran while one was open for 21% -> 28% of each run, Pallas kernels for 0% -> 0%
where the time goes in v1:
time: 1220 us; the launch traced here: 1210 us
  waiting for transfers between devices  529 us (43%)
  matrix products  238 us (20%)
  other arithmetic  207 us (17%)
  local copies, waits for them, and re-layouts  156 us (13%)
  starting transfers between devices  73.3 us (6%)
    ppermute x89, waiting for transfers between devices, swap(): lax.ppermute(values, axis_name, [(i, i ^ 1 << bit) for i in range(size)])  529 us
    ppermute x89, starting transfers between devices, swap(): lax.ppermute(values, axis_name, [(i, i ^ 1 << bit) for i in range(size)])  73.3 us
    dot_general x7, matrix products, back_product(): lax.dot_general(left_side, right_side, (((1,), (1,)), ((), ())), preferre...  47.5 us
    dot_general x7, matrix products, product(): return jnp.dot(left_side, right_side, preferred_element_type=jnp.float32)  45.7 us
    dot_general x7, matrix products, outer_sum(): lax.dot_general(left_side, right_side, (((0,), (0,)), ((), ())), preferre...  45.5 us
    unnamed x218, local copies, waits for them, and re-layouts  39.5 us
    convert_element_type x28, other arithmetic, exchange_sum_scatter(): held = total.astype(last if step == bits - 1 else values.dtype)  39.3 us
    select_n x42, other arithmetic, exchange_gather(): jnp.where(upper, other, held)  39.2 us
  transfers between devices with their start and end apart: 89, of which 38 were waited for; matrix products, arithmetic and copies ran while one was open for 28% of the time, Pallas kernels for 0%

profile of v1, /device:TPU:0, one launch (start us, length us, event | category | flops | bytes accessed | tf_op | source)
XLA Modules:
  0.0 1206.9 jit_solution(17357296567371171741)
XLA Ops:
  65.4 20.7 %collective-permute-done.37 = bf16[1,1,2,1,72,1152]{5,4,3,2,1,0:T(8,128)(2,1)S(1)} collective-permute-done((bf16[1,1,2,1,72,1152]{5,4,3,2,1,0:T(8,128)(2,1)S(1)}, bf16[1,1,2,1,72,1152]{5,4,3,2,1,0:T(8,128)(2,1)S(1)}, u32[]{:S(2)}, u32[]{:S(2)}) %collective-permute-start.37) | collective-permute-done | bytes 331808 | tf_op jit(solution)/shard_map/ppermute | solution.py:130
  92.2 24.9 %collective-permute-done.34 = bf16[1,1,2,2,72,1152]{5,4,3,2,1,0:T(8,128)(2,1)S(1)} collective-permute-done((bf16[1,1,2,2,72,1152]{5,4,3,2,1,0:T(8,128)(2,1)S(1)}, bf16[1,1,2,2,72,1152]{5,4,3,2,1,0:T(8,128)(2,1)S(1)}, u32[]{:S(2)}, u32[]{:S(2)}) %collective-permute-start.34) | collective-permute-done | bytes 663584 | tf_op jit(solution)/shard_map/ppermute | solution.py:130
  117.3 12.8 %collective-permute-done.38 = bf16[1,2,2,1,72,1152]{5,4,3,2,1,0:T(8,128)(2,1)S(1)} collective-permute-done((bf16[1,2,2,1,72,1152]{5,4,3,2,1,0:T(8,128)(2,1)S(1)}, bf16[1,2,2,1,72,1152]{5,4,3,2,1,0:T(8,128)(2,1)S(1)}, u32[]{:S(2)}, u32[]{:S(2)}) %collective-permute-start.38) | collective-permute-done | bytes 663584 | tf_op jit(solution)/shard_map/ppermute | solution.py:130
  142.2 49.0 %collective-permute-done.10 = bf16[1,2,2,1,72,1152]{5,4,3,2,1,0:T(8,128)(2,1)S(1)} collective-permute-done((bf16[1,2,2,1,72,1152]{5,4,3,2,1,0:T(8,128)(2,1)S(1)}, bf16[1,2,2,1,72,1152]{5,4,3,2,1,0:T(8,128)(2,1)S(1)}, u32[]{:S(2)}, u32[]{:S(2)}) %collective-permute-start.10) | collective-permute-done | bytes 663584 | tf_op jit(solution)/shard_map/ppermute | solution.py:130
  210.8 12.9 %collective-permute-done.11 = bf16[2,2,2,1,72,1152]{5,4,3,2,1,0:T(8,128)(2,1)S(1)} collective-permute-done((bf16[2,2,2,1,72,1152]{5,4,3,2,1,0:T(8,128)(2,1)S(1)}, bf16[2,2,2,1,72,1152]{5,4,3,2,1,0:T(8,128)(2,1)S(1)}, u32[]{:S(2)}, u32[]{:S(2)}) %collective-permute-start.11) | collective-permute-done | bytes 1327136 | tf_op jit(solution)/shard_map/ppermute | solution.py:130
  226.7 63.6 %collective-permute-done.7 = bf16[1,2,2,2,72,1152]{5,4,3,2,1,0:T(8,128)(2,1)S(1)} collective-permute-done((bf16[1,2,2,2,72,1152]{5,4,3,2,1,0:T(8,128)(2,1)S(1)}, bf16[1,2,2,2,72,1152]{5,4,3,2,1,0:T(8,128)(2,1)S(1)}, u32[]{:S(2)}, u32[]{:S(2)}) %collective-permute-start.7) | collective-permute-done | bytes 1327136 | tf_op jit(solution)/shard_map/ppermute | solution.py:130
  303.3 22.7 %collective-permute-done.21 = bf16[1,2,2,2,72,1152]{5,4,3,2,1,0:T(8,128)(2,1)} collective-permute-done((bf16[1,2,2,2,72,1152]{5,4,3,2,1,0:T(8,128)(2,1)}, bf16[1,2,2,2,72,1152]{5,4,3,2,1,0:T(8,128)(2,1)}, u32[]{:S(2)}, u32[]{:S(2)}) %collective-permute-start.21) | collective-permute-done | bytes 1327136 | tf_op jit(solution)/shard_map/ppermute | solution.py:130
  438.1 14.9 %multiply_reduce_fusion.1 = (f32[16,512]{1,0:T(8,128)S(1)}, f32[16,512,1024]{2,1,0:T(8,128)}) fusion(bf16[512,16,72]{0,2,1:T(8,128)(2,1)} %bitcast.499, bf16[1024,16,72]{0,2,1:T(8,128)(2,1)S(1)} %bitcast.481), kind=kOutput, calls=%fused_computation.6 | convolution fusion | flops 1224728576 | bytes 37126144 | tf_op jit(solution)/shard_map/sqhd,skhd->shqk/dot_general | solution.py:51
  453.0 14.4 %fusion = f32[16,512]{1,0:T(8,128)S(1)} fusion(f32[16,512,1024]{2,1,0:T(8,128)} %get-tuple-element.206, f32[16,512]{1,0:T(8,128)S(1)} %get-tuple-element.205), kind=kLoop, calls=%fused_computation.5 | loop fusion | flops 25157632 | bytes 33619968 | tf_op jit(solution)/shard_map/reduce_sum | solution.py:63
  468.0 13.4 %fusion.56 = bf16[16,72,512]{2,1,0:T(8,128)(2,1)S(1)} fusion(bf16[1024,16,72]{0,2,1:T(8,128)(2,1)S(1)} %bitcast.502, f32[16,512,1024]{2,1,0:T(8,128)} %get-tuple-element.206, f32[16,512]{1,0:T(8,128)S(1)} %fusion, f32[16,512]{1,0:T(8,128)S(1)} %get-tuple-element.205), kind=kOutput, calls=%fused_computation.161 | convolution fusion | flops 1242103808 | bytes 37158912 | tf_op jit(solution)/shard_map/shqk,skhd->sqhd/dot_general | solution.py:66
  503.7 13.6 %fusion.54 = f32[512,4608]{1,0:T(8,128)} fusion(bf16[1152,1152]{1,0:T(8,128)(2,1)} %bitcast.564, bf16[1152,1152]{1,0:T(8,128)(2,1)} %bitcast.566, bf16[1152,1152]{1,0:T(8,128)(2,1)} %bitcast.568, bf16[1152,1152]{1,0:T(8,128)(2,1)S(1)} %bitcast.562, f32[1,512,1152]{2,1,0:T(8,128)} %copy-done.59, f32[1152]{0:T(1024)S(1)} %copy-done.90, ...), kind=kOutput, calls=%fused_computation.159 | convolution fusion | flops 5481234432 | bytes 22426624 | tf_op jit(solution)/shard_map/dot_general | solution.py:31
  517.3 13.0 %convolution_convert_fusion = bf16[4608,1152]{1,0:T(8,128)(2,1)} fusion(bf16[1,512,1152]{2,1,0:T(8,128)(2,1)S(1)} %copy-done.67, f32[1152]{0:T(1024)S(1)} %copy-done.92, f32[512,4608]{1,0:T(8,128)} %fusion.54), kind=kOutput, calls=%fused_computation.8 | convolution fusion | flops 5464129536 | bytes 21238272 | tf_op jit(solution)/shard_map/dot_general | solution.py:35
  530.3 16.2 %fusion.15 = bf16[512,4608]{1,0:T(8,128)(2,1)} fusion(f32[512,4608]{1,0:T(8,128)} %fusion.54, bf16[4608,1152]{1,0:T(8,128)(2,1)} %bitcast.511, bf16[1,512,1152]{2,1,0:T(8,128)(2,1)S(1)} %copy-done.67, f32[1152]{0:T(1024)S(1)} %copy-done.92), kind=kOutput, calls=%fused_computation.40 | convolution fusion | flops 5484773376 | bytes 25956864 | tf_op jit(solution)/shard_map/dot_general | solution.py:41
  546.5 12.6 %fusion.42 = (f32[1152]{0:T(1024)S(1)}, f32[512]{0:T(512)S(1)}, f32[512,1152]{1,0:T(8,128)}) fusion(f32[1,512,1152]{2,1,0:T(8,128)} %copy-done.59, f32[512]{0:T(512)S(1)} %fusion.86, f32[512]{0:T(512)S(1)} %broadcast_multiply_fusion, f32[1152]{0:T(1024)S(1)} %copy-done.91, bf16[512,4608]{1,0:T(8,128)(2,1)} %fusion.15, bf16[1152,1152]{1,0:T(8,128)(2,1)} %bitcast.565, ...), kind=kOutput, calls=%fused_computation.135 | convolution fusion | flops 5482412544 | bytes 20069376 | tf_op jit(solution)/shard_map/dot_general | solution.py:41
  606.3 15.9 %convert_bitcast_fusion = bf16[1,1024,16,72]{1,3,2,0:T(8,128)(2,1)} fusion(bf16[512,16,72]{0,2,1:T(8,128)(2,1)} %bitcast.504, f32[16,512,1024]{2,1,0:T(8,128)} %get-tuple-element.206, f32[16,512]{1,0:T(8,128)S(1)} %copy-done.74), kind=kOutput, calls=%fused_computation.145 | convolution fusion | flops 1234305024 | bytes 37126144 | tf_op jit(solution)/shard_map/shqk,sqhd->skhd/dot_general | solution.py:87
  622.1 24.3 %multiply_reduce_fusion = (f32[16,512]{1,0:T(8,128)S(1)}, f32[16,512,1024]{2,1,0:T(8,128)}) fusion(f32[16,512,1024]{2,1,0:T(8,128)} %get-tuple-element.206, f32[16,512]{1,0:T(8,128)S(1)} %copy-done.74, bf16[512,16,72]{0,2,1:T(8,128)(2,1)} %bitcast.505, bf16[1024,16,72]{0,2,1:T(8,128)(2,1)S(1)} %bitcast.503), kind=kOutput, calls=%fused_computation.1 | convolution fusion | flops 1241505792 | bytes 70713344 | tf_op jit(solution)/shard_map/sqhd,skhd->shqk/dot_general | solution.py:74
  703.2 28.0 %multiply_convert_fusion = bf16[16,512,1024]{2,1,0:T(8,128)(2,1)} fusion(f32[16,512,1024]{2,1,0:T(8,128)} %get-tuple-element.215, f32[16,512,1024]{2,1,0:T(8,128)} %get-tuple-element.206, f32[16,512]{1,0:T(8,128)S(1)} %get-tuple-element.214, f32[16,512]{1,0:T(8,128)S(1)} %copy-done.74), kind=kLoop, calls=%fused_computation | loop fusion | flops 41943040 | bytes 83951616 | tf_op jit(solution)/shard_map/convert_element_type | solution.py:81
  891.7 46.8 %collective-permute-done.80 = bf16[1,2,2,2,72,1152]{5,4,3,2,1,0:T(8,128)(2,1)} collective-permute-done((bf16[1,2,2,2,72,1152]{5,4,3,2,1,0:T(8,128)(2,1)}, bf16[1,2,2,2,72,1152]{5,4,3,2,1,0:T(8,128)(2,1)}, u32[]{:S(2)}, u32[]{:S(2)}) %collective-permute-start.80) | collective-permute-done | bytes 1327136 | tf_op jit(solution)/shard_map/ppermute | solution.py:130
  947.7 47.7 %collective-permute-done.74 = bf16[1,2,2,2,72,1152]{5,4,3,2,1,0:T(8,128)(2,1)} collective-permute-done((bf16[1,2,2,2,72,1152]{5,4,3,2,1,0:T(8,128)(2,1)}, bf16[1,2,2,2,72,1152]{5,4,3,2,1,0:T(8,128)(2,1)}, u32[]{:S(2)}, u32[]{:S(2)}) %collective-permute-start.74) | collective-permute-done | bytes 1327136 | tf_op jit(solution)/shard_map/ppermute | solution.py:130
  998.2 53.9 %collective-permute-done.85 = bf16[1,2,2,1,72,1152]{5,4,3,2,1,0:T(8,128)(2,1)S(1)} collective-permute-done((bf16[1,2,2,1,72,1152]{5,4,3,2,1,0:T(8,128)(2,1)S(1)}, bf16[1,2,2,1,72,1152]{5,4,3,2,1,0:T(8,128)(2,1)S(1)}, u32[]{:S(2)}, u32[]{:S(2)}) %collective-permute-start.85) | collective-permute-done | bytes 663584 | tf_op jit(solution)/shard_map/ppermute | solution.py:130
  1053.4 15.6 %collective-permute-done.75 = bf16[1,1,2,2,72,1152]{5,4,3,2,1,0:T(8,128)(2,1)S(1)} collective-permute-done((bf16[1,1,2,2,72,1152]{5,4,3,2,1,0:T(8,128)(2,1)S(1)}, bf16[1,1,2,2,72,1152]{5,4,3,2,1,0:T(8,128)(2,1)S(1)}, u32[]{:S(2)}, u32[]{:S(2)}) %collective-permute-start.75) | collective-permute-done | bytes 663584 | tf_op jit(solution)/shard_map/ppermute | solution.py:130
  1085.8 15.0 %collective-permute-done.72 = bf16[1,2,1,1,72,1152]{5,4,3,2,1,0:T(8,128)(2,1)S(1)} collective-permute-done((bf16[1,2,1,1,72,1152]{5,4,3,2,1,0:T(8,128)(2,1)S(1)}, bf16[1,2,1,1,72,1152]{5,4,3,2,1,0:T(8,128)(2,1)S(1)}, u32[]{:S(2)}, u32[]{:S(2)}) %collective-permute-start.72) | collective-permute-done | bytes 331808 | tf_op jit(solution)/shard_map/ppermute | solution.py:130
  1124.7 20.3 %collective-permute-done.61 = bf16[1,2,2,1,72,1152]{5,4,3,2,1,0:T(8,128)(2,1)S(1)} collective-permute-done((bf16[1,2,2,1,72,1152]{5,4,3,2,1,0:T(8,128)(2,1)S(1)}, bf16[1,2,2,1,72,1152]{5,4,3,2,1,0:T(8,128)(2,1)S(1)}, u32[]{:S(2)}, u32[]{:S(2)}) %collective-permute-start.61) | collective-permute-done | bytes 663584 | tf_op jit(solution)/shard_map/ppermute | solution.py:130
  1155.5 26.3 %collective-permute-done.55 = bf16[1,2,2,1,72,1152]{5,4,3,2,1,0:T(8,128)(2,1)S(1)} collective-permute-done((bf16[1,2,2,1,72,1152]{5,4,3,2,1,0:T(8,128)(2,1)S(1)}, bf16[1,2,2,1,72,1152]{5,4,3,2,1,0:T(8,128)(2,1)S(1)}, u32[]{:S(2)}, u32[]{:S(2)}) %collective-permute-start.55) | collective-permute-done | bytes 663584 | tf_op jit(solution)/shard_map/ppermute | solution.py:130
  (683 shorter events, 605.1 us)
Async XLA Ops:
  89.7 107.0 %collective-permute-start.29 = (bf16[2,2,1,1,72,1152]{5,4,3,2,1,0:T(8,128)(2,1)S(1)}, bf16[2,2,1,1,72,1152]{5,4,3,2,1,0:T(8,128)(2,1)S(1)}, u32[]{:S(2)}, u32[]{:S(2)}) collective-permute-start(bf16[2,2,1,1,72,1152]{5,4,3,2,1,0:T(8,128)(2,1)S(1)} %pad_maximum_fusion.56), channel_id=1, source_target_pairs={{0,2},{2,0},{4,6},{6,4},{8,10},{10,8},{12,14},{14,12},{16,18},{18,... | collective-permute-start | bytes 1990664 | tf_op jit(solution)/shard_map/ppermute | solution.py:130
  89.8 106.9 %collective-permute-start.16 = (bf16[2,2,1,1,72,1152]{5,4,3,2,1,0:T(8,128)(2,1)S(1)}, bf16[2,2,1,1,72,1152]{5,4,3,2,1,0:T(8,128)(2,1)S(1)}, u32[]{:S(2)}, u32[]{:S(2)}) collective-permute-start(bf16[2,2,1,1,72,1152]{5,4,3,2,1,0:T(8,128)(2,1)S(1)} %pad_maximum_fusion.52), channel_id=1, source_target_pairs={{0,2},{2,0},{4,6},{6,4},{8,10},{10,8},{12,14},{14,12},{16,18},{18,... | collective-permute-start | bytes 1990664 | tf_op jit(solution)/shard_map/ppermute | solution.py:130
  117.2 74.5 %collective-permute-start.6 = (bf16[1,1,2,2,72,1152]{5,4,3,2,1,0:T(8,128)(2,1)S(1)}, bf16[1,1,2,2,72,1152]{5,4,3,2,1,0:T(8,128)(2,1)S(1)}, u32[]{:S(2)}, u32[]{:S(2)}) collective-permute-start(bf16[1,1,2,2,72,1152]{5,4,3,2,1,0:T(8,128)(2,1)S(1)} %pad_maximum_fusion.49), channel_id=1, source_target_pairs={{0,8},{2,10},{4,12},{6,14},{8,0},{10,2},{12,4},{14,6},{16,24},{18,... | collective-permute-start | bytes 1990664 | tf_op jit(solution)/shard_map/ppermute | solution.py:130
  130.1 61.1 %collective-permute-start.10 = (bf16[1,2,2,1,72,1152]{5,4,3,2,1,0:T(8,128)(2,1)S(1)}, bf16[1,2,2,1,72,1152]{5,4,3,2,1,0:T(8,128)(2,1)S(1)}, u32[]{:S(2)}, u32[]{:S(2)}) collective-permute-start(bf16[1,2,2,1,72,1152]{5,4,3,2,1,0:T(8,128)(2,1)S(1)} %pad_maximum_fusion.50), channel_id=1, source_target_pairs={{0,16},{2,18},{4,20},{6,22},{8,24},{10,26},{12,28},{14,30},{16,0},... | collective-permute-start | bytes 1990664 | tf_op jit(solution)/shard_map/ppermute | solution.py:130
  191.2 102.7 %collective-permute-start.35 = (bf16[1,2,2,2,72,1152]{5,4,3,2,1,0:T(8,128)(2,1)S(1)}, bf16[1,2,2,2,72,1152]{5,4,3,2,1,0:T(8,128)(2,1)}, u32[]{:S(2)}, u32[]{:S(2)}) collective-permute-start(bf16[1,2,2,2,72,1152]{5,4,3,2,1,0:T(8,128)(2,1)S(1)} %pad_maximum_fusion.38), channel_id=1, source_target_pairs={{0,16},{2,18},{4,20},{6,22},{8,24},{10,26},{12,28},{14,30},{16,0},... | collective-permute-start | bytes 3981320 | tf_op jit(solution)/shard_map/ppermute | solution.py:130
  196.7 98.8 %collective-permute-start.39 = (bf16[2,2,2,1,72,1152]{5,4,3,2,1,0:T(8,128)(2,1)}, bf16[2,2,2,1,72,1152]{5,4,3,2,1,0:T(8,128)(2,1)}, u32[]{:S(2)}, u32[]{:S(2)}) collective-permute-start(bf16[2,2,2,1,72,1152]{5,4,3,2,1,0:T(8,128)(2,1)} %pad_maximum_fusion.39), channel_id=1, source_target_pairs={{0,2},{2,0},{4,6},{6,4},{8,10},{10,8},{12,14},{14,12},{16,18},{18,... | collective-permute-start | bytes 3981320 | tf_op jit(solution)/shard_map/ppermute | solution.py:130
  196.7 93.5 %collective-permute-start.7 = (bf16[1,2,2,2,72,1152]{5,4,3,2,1,0:T(8,128)(2,1)S(1)}, bf16[1,2,2,2,72,1152]{5,4,3,2,1,0:T(8,128)(2,1)S(1)}, u32[]{:S(2)}, u32[]{:S(2)}) collective-permute-start(bf16[1,2,2,2,72,1152]{5,4,3,2,1,0:T(8,128)(2,1)S(1)} %pad_maximum_fusion.32), channel_id=1, source_target_pairs={{0,16},{2,18},{4,20},{6,22},{8,24},{10,26},{12,28},{14,30},{16,0},... | collective-permute-start | bytes 3981320 | tf_op jit(solution)/shard_map/ppermute | solution.py:130
  209.5 91.9 %collective-permute-start.17 = (bf16[2,2,1,2,72,1152]{5,4,3,2,1,0:T(8,128)(2,1)}, bf16[2,2,1,2,72,1152]{5,4,3,2,1,0:T(8,128)(2,1)}, u32[]{:S(2)}, u32[]{:S(2)}) collective-permute-start(bf16[2,2,1,2,72,1152]{5,4,3,2,1,0:T(8,128)(2,1)} %pad_maximum_fusion.34), channel_id=1, source_target_pairs={{0,4},{2,6},{4,0},{6,2},{8,12},{10,14},{12,8},{14,10},{16,20},{18,... | collective-permute-start | bytes 3981320 | tf_op jit(solution)/shard_map/ppermute | solution.py:130
  223.8 107.5 %collective-permute-start.30 = (bf16[2,2,1,2,72,1152]{5,4,3,2,1,0:T(8,128)(2,1)}, bf16[2,2,1,2,72,1152]{5,4,3,2,1,0:T(8,128)(2,1)}, u32[]{:S(2)}, u32[]{:S(2)}) collective-permute-start(bf16[2,2,1,2,72,1152]{5,4,3,2,1,0:T(8,128)(2,1)} %pad_maximum_fusion.37), channel_id=1, source_target_pairs={{0,4},{2,6},{4,0},{6,2},{8,12},{10,14},{12,8},{14,10},{16,20},{18,... | collective-permute-start | bytes 3981320 | tf_op jit(solution)/shard_map/ppermute | solution.py:130
  300.9 66.1 %collective-permute-start.40 = (bf16[1,2,16,72,1152]{4,3,2,1,0:T(8,128)(2,1)}, bf16[1,2,16,72,1152]{4,3,2,1,0:T(8,128)(2,1)}, u32[]{:S(2)}, u32[]{:S(2)}) collective-permute-start(bf16[1,2,16,72,1152]{4,3,2,1,0:T(8,128)(2,1)} %maximum_bitcast_fusion.3), channel_id=1, source_target_pairs={{0,1},{1,0},{2,3},{3,2},{4,5},{5,4},{6,7},{7,6},{8,9},{9,8},{10,11... | collective-permute-start | bytes 15925256 | tf_op jit(solution)/shard_map/ppermute | solution.py:130
  331.2 65.2 %collective-permute-start.22 = (bf16[1,2,16,72,1152]{4,3,2,1,0:T(8,128)(2,1)}, bf16[1,2,16,72,1152]{4,3,2,1,0:T(8,128)(2,1)}, u32[]{:S(2)}, u32[]{:S(2)}) collective-permute-start(bf16[1,2,16,72,1152]{4,3,2,1,0:T(8,128)(2,1)} %maximum_bitcast_fusion.1), channel_id=1, source_target_pairs={{0,1},{1,0},{2,3},{3,2},{4,5},{5,4},{6,7},{7,6},{8,9},{9,8},{10,11... | collective-permute-start | bytes 15925256 | tf_op jit(solution)/shard_map/ppermute | solution.py:130
  661.0 106.0 %collective-permute-start.43 = (f32[1,120,2304]{2,1,0:T(8,128)}, f32[1,120,2304]{2,1,0:T(8,128)}, u32[]{:S(2)}, u32[]{:S(2)}) collective-permute-start(f32[1,120,2304]{2,1,0:T(8,128)} %pad_maximum_fusion.46), channel_id=1, source_target_pairs={{0,1},{1,0},{2,3},{3,2},{4,5},{5,4},{6,7},{7,6},{8,9},{9,8},{10,11... | collective-permute-start | bytes 3317768 | tf_op jit(solution)/shard_map/ppermute | solution.py:130
  679.2 105.2 %collective-permute-start.42 = (bf16[1,1,512,1152]{2,3,1,0:T(8,128)(2,1)}, bf16[1,1,512,1152]{2,3,1,0:T(8,128)(2,1)}, u32[]{:S(2)}, u32[]{:S(2)}) collective-permute-start(bf16[1,1,512,1152]{2,3,1,0:T(8,128)(2,1)} %copy.93), channel_id=1, source_target_pairs={{0,1},{1,0},{2,3},{3,2},{4,5},{5,4},{6,7},{7,6},{8,9},{9,8},{10,11... | collective-permute-start | bytes 3538952 | tf_op jit(solution)/shard_map/ppermute | solution.py:130
  702.7 135.1 %collective-permute-start.79 = (bf16[1,2,16,72,1152]{4,3,2,1,0:T(8,128)(2,1)}, bf16[1,2,16,72,1152]{4,3,2,1,0:T(8,128)(2,1)}, u32[]{:S(2)}, u32[]{:S(2)}) collective-permute-start(bf16[1,2,16,72,1152]{4,3,2,1,0:T(8,128)(2,1)} %constant_dynamic-slice_fusion.8), channel_id=1, source_target_pairs={{0,1},{1,0},{2,3},{3,2},{4,5},{5,4},{6,7},{7,6},{8,9},{9,8},{10,11... | collective-permute-start | bytes 15925256 | tf_op jit(solution)/shard_map/ppermute | solution.py:130
  702.8 149.6 %collective-permute-start.69 = (bf16[1,2,16,72,1152]{4,3,2,1,0:T(8,128)(2,1)}, bf16[1,2,16,72,1152]{4,3,2,1,0:T(8,128)(2,1)}, u32[]{:S(2)}, u32[]{:S(2)}) collective-permute-start(bf16[1,2,16,72,1152]{4,3,2,1,0:T(8,128)(2,1)} %constant_dynamic-slice_fusion.17), channel_id=1, source_target_pairs={{0,1},{1,0},{2,3},{3,2},{4,5},{5,4},{6,7},{7,6},{8,9},{9,8},{10,11... | collective-permute-start | bytes 15925256 | tf_op jit(solution)/shard_map/ppermute | solution.py:130
  781.7 84.1 %collective-permute-start.59 = (bf16[1,2,16,72,1152]{4,3,2,1,0:T(8,128)(2,1)}, bf16[1,2,16,72,1152]{4,3,2,1,0:T(8,128)(2,1)}, u32[]{:S(2)}, u32[]{:S(2)}) collective-permute-start(bf16[1,2,16,72,1152]{4,3,2,1,0:T(8,128)(2,1)} %constant_dynamic-slice_fusion.26), channel_id=1, source_target_pairs={{0,1},{1,0},{2,3},{3,2},{4,5},{5,4},{6,7},{7,6},{8,9},{9,8},{10,11... | collective-permute-start | bytes 15925256 | tf_op jit(solution)/shard_map/ppermute | solution.py:130
  850.0 88.5 %collective-permute-start.80 = (bf16[1,2,2,2,72,1152]{5,4,3,2,1,0:T(8,128)(2,1)}, bf16[1,2,2,2,72,1152]{5,4,3,2,1,0:T(8,128)(2,1)}, u32[]{:S(2)}, u32[]{:S(2)}) collective-permute-start(bf16[1,2,2,2,72,1152]{5,4,3,2,1,0:T(8,128)(2,1)} %constant_dynamic-slice_fusion.7), channel_id=1, source_target_pairs={{0,16},{2,18},{4,20},{6,22},{8,24},{10,26},{12,28},{14,30},{16,0},... | collective-permute-start | bytes 3981320 | tf_op jit(solution)/shard_map/ppermute | solution.py:130
  852.3 88.9 %collective-permute-start.84 = (bf16[2,2,2,1,72,1152]{5,4,3,2,1,0:T(8,128)(2,1)}, bf16[2,2,2,1,72,1152]{5,4,3,2,1,0:T(8,128)(2,1)}, u32[]{:S(2)}, u32[]{:S(2)}) collective-permute-start(bf16[2,2,2,1,72,1152]{5,4,3,2,1,0:T(8,128)(2,1)} %constant_dynamic-slice_fusion.3), channel_id=1, source_target_pairs={{0,2},{2,0},{4,6},{6,4},{8,10},{10,8},{12,14},{14,12},{16,18},{18,... | collective-permute-start | bytes 3981320 | tf_op jit(solution)/shard_map/ppermute | solution.py:130
  862.8 80.4 %collective-permute-start.70 = (bf16[2,2,1,2,72,1152]{5,4,3,2,1,0:T(8,128)(2,1)}, bf16[2,2,1,2,72,1152]{5,4,3,2,1,0:T(8,128)(2,1)}, u32[]{:S(2)}, u32[]{:S(2)}) collective-permute-start(bf16[2,2,1,2,72,1152]{5,4,3,2,1,0:T(8,128)(2,1)} %constant_dynamic-slice_fusion.16), channel_id=1, source_target_pairs={{0,4},{2,6},{4,0},{6,2},{8,12},{10,14},{12,8},{14,10},{16,20},{18,... | collective-permute-start | bytes 3981320 | tf_op jit(solution)/shard_map/ppermute | solution.py:130
  865.8 129.6 %collective-permute-start.74 = (bf16[1,2,2,2,72,1152]{5,4,3,2,1,0:T(8,128)(2,1)}, bf16[1,2,2,2,72,1152]{5,4,3,2,1,0:T(8,128)(2,1)}, u32[]{:S(2)}, u32[]{:S(2)}) collective-permute-start(bf16[1,2,2,2,72,1152]{5,4,3,2,1,0:T(8,128)(2,1)} %constant_dynamic-slice_fusion.12), channel_id=1, source_target_pairs={{0,16},{2,18},{4,20},{6,22},{8,24},{10,26},{12,28},{14,30},{16,0},... | collective-permute-start | bytes 3981320 | tf_op jit(solution)/shard_map/ppermute | solution.py:130
  881.0 229.0 %collective-permute-start.60 = (bf16[2,2,2,1,72,1152]{5,4,3,2,1,0:T(8,128)(2,1)}, bf16[2,2,2,1,72,1152]{5,4,3,2,1,0:T(8,128)(2,1)}, u32[]{:S(2)}, u32[]{:S(2)}) collective-permute-start(bf16[2,2,2,1,72,1152]{5,4,3,2,1,0:T(8,128)(2,1)} %constant_dynamic-slice_fusion.25), channel_id=1, source_target_pairs={{0,2},{2,0},{4,6},{6,4},{8,10},{10,8},{12,14},{14,12},{16,18},{18,... | collective-permute-start | bytes 3981320 | tf_op jit(solution)/shard_map/ppermute | solution.py:130
  938.5 174.8 %collective-permute-start.64 = (bf16[2,2,1,2,72,1152]{5,4,3,2,1,0:T(8,128)(2,1)S(1)}, bf16[2,2,1,2,72,1152]{5,4,3,2,1,0:T(8,128)(2,1)S(1)}, u32[]{:S(2)}, u32[]{:S(2)}) collective-permute-start(bf16[2,2,1,2,72,1152]{5,4,3,2,1,0:T(8,128)(2,1)S(1)} %copy-done.65), channel_id=1, source_target_pairs={{0,4},{2,6},{4,0},{6,2},{8,12},{10,14},{12,8},{14,10},{16,20},{18,... | collective-permute-start | bytes 3981320 | tf_op jit(solution)/shard_map/ppermute | solution.py:130
  941.2 181.2 %collective-permute-start.50 = (bf16[1,2,2,2,72,1152]{5,4,3,2,1,0:T(8,128)(2,1)S(1)}, bf16[1,2,2,2,72,1152]{5,4,3,2,1,0:T(8,128)(2,1)S(1)}, u32[]{:S(2)}, u32[]{:S(2)}) collective-permute-start(bf16[1,2,2,2,72,1152]{5,4,3,2,1,0:T(8,128)(2,1)S(1)} %constant_dynamic-slice_fusion.34), channel_id=1, source_target_pairs={{0,16},{2,18},{4,20},{6,22},{8,24},{10,26},{12,28},{14,30},{16,0},... | collective-permute-start | bytes 3981320 | tf_op jit(solution)/shard_map/ppermute | solution.py:130
  1052.3 71.1 %collective-permute-start.54 = (bf16[2,2,2,1,72,1152]{5,4,3,2,1,0:T(8,128)(2,1)S(1)}, bf16[2,2,2,1,72,1152]{5,4,3,2,1,0:T(8,128)(2,1)S(1)}, u32[]{:S(2)}, u32[]{:S(2)}) collective-permute-start(bf16[2,2,2,1,72,1152]{5,4,3,2,1,0:T(8,128)(2,1)S(1)} %constant_dynamic-slice_fusion.30), channel_id=1, source_target_pairs={{0,2},{2,0},{4,6},{6,4},{8,10},{10,8},{12,14},{14,12},{16,18},{18,... | collective-permute-start | bytes 3981320 | tf_op jit(solution)/shard_map/ppermute | solution.py:130
  (172 other events, 4125.2 us)
